TPU v7x, 256 devices: a whole 4x4x8 slice. The times are simulated.
256 devices in a mesh: blk: 64 (over y, z, core), rep: 4 (over x).
Axes of the slice: x: 4, y: 4, z: 8, core: 2. Of those that a mesh axis runs over, the one named last changes fastest.
Arguments:
- sim: bfloat16 [131072, 512], P(('blk', 'rep')), may hold values from -48 to 48, as said below
- real: bfloat16 [131072, 512], P('blk', 'rep'), may hold values from -48 to 48, as said below
- pair_real: int32 [512, 16], P(('blk', 'rep')), may hold values from 0 to 511, as said below
- pair_count: int32 [512], P(('blk', 'rep')), may hold values from 2 to 16, as said below
Outputs:
- pull: float32 [131072, 512], P(('blk', 'rep'))
- sim_potential: float32 [131072], P(('blk', 'rep'))
- real_potential: float32 [131072], P('blk')
Inputs may be any that keep to these rules, and one draw needn't show every extreme that they name: `sim`: clipped normal values; the row scales differ between draws. `real`: clipped normal values; the row scales differ between draws. pair_real[s, k] lies in the real blocks of the blk indices next to or equal to that of evolved block s, that is from 8 * (s // 8) - 8 to 8 * (s // 8) + 2 * 8 - 1, within the grid; the entries of one row are distinct; pair_real[s, 0] = s; slots k >= pair_count[s] hold valid but unused numbers. `pair_count`: some evolved block has all 16 slots used in every draw.
All inputs are finite; a program needn't handle non-finite values.
Results may differ from a plain program's by a relative error of at most 0.0085.
Values may be sent and summed in bfloat16 or wider, within the bound.
No kernel may reach another device: no remote copies, remote signals or barrier semaphores. Data moves between devices by JAX's collectives and lax.ppermute only.
A program may use at most 128 MiB of HBM per device.

v0:
```python
import math

import jax
import jax.numpy as jnp
from jax import lax
from jax.sharding import PartitionSpec as P

BLOCK_ROWS = 256
ITERS = 3


EPS = 0.05
NEG = -1e30


def with_halo(block, sides, width):
    for axis, dim in sides:
        count = lax.axis_size(axis)
        forward = [(i, i + 1) for i in range(count - 1)]
        backward = [(target, source) for source, target in forward]
        low = lax.ppermute(
            lax.slice_in_dim(block, block.shape[dim] - width, None, axis=dim), axis, forward
        )
        high = lax.ppermute(lax.slice_in_dim(block, 0, width, axis=dim), axis, backward)
        block = jnp.concatenate([low, block, high], axis=dim)
    return block


def joined(value, axis, join):
    pieces = jax.tree.map(lambda part: lax.all_gather(part, axis), value)
    head = jax.tree.map(lambda part: part[0], pieces)
    tail = jax.tree.map(lambda part: part[1:], pieces)
    so_far, _ = lax.scan(lambda so_far, piece: (join(so_far, piece), None), head, tail)
    return so_far


def passed_along(value, axis, by):
    devices = lax.axis_size(axis)
    pairs = [(i, i + by) for i in range(devices) if 0 <= i + by < devices]
    return lax.ppermute(value, axis, pairs)


def combine(former, latter):
    highest = jnp.maximum(former[0], latter[0])
    return (
        highest,
        former[1] * jnp.exp(former[0] - highest) + latter[1] * jnp.exp(latter[0] - highest),
    )


def guarded(stats):
    return (jnp.where(stats[1] > 0.0, stats[0], NEG), stats[1])


def shards(sim, real, pair_real, pair_count):
    replicas = lax.axis_size("rep")
    owners = lax.axis_size("blk")
    tile_rows = BLOCK_ROWS
    features = sim.shape[1]
    real_local = real.shape[0] // tile_rows
    window_count = 3 * real_local
    rows_total = float(owners * replicas * sim.shape[0])
    log_rows = math.log(rows_total)
    whole = lax.all_gather(real, "rep", axis=1, tiled=True)
    window = with_halo(whole, (("blk", 0),), real.shape[0])
    window = window.reshape(window_count, tile_rows, features)
    sim_count = pair_count.shape[0]
    fan_slots = pair_real.shape[1]
    slots = pair_real.shape[0] * fan_slots
    base = (lax.axis_index("blk") - 1) * real_local
    table_window = jnp.clip(pair_real - base, 0, window_count - 1).reshape(-1)
    table_sim = jnp.repeat(jnp.arange(sim_count, dtype=jnp.int32), fan_slots)
    table_active = (jnp.arange(fan_slots)[None, :] < pair_count[:, None]).reshape(-1)
    order = jnp.argsort(jnp.where(table_active, 0, 1).astype(jnp.int32), stable=True)
    active_total = jnp.sum(table_active.astype(jnp.int32))
    slot_window = table_window[order]
    slot_sim = table_sim[order]
    alive = jnp.arange(slots) < active_total
    sim_tiles = sim.reshape(sim_count, tile_rows, features)
    sim_norm = jnp.sum(jnp.square(sim_tiles.astype(jnp.float32)), -1)
    real_norm = jnp.sum(jnp.square(window.astype(jnp.float32)), -1)
    group_size = 4
    rounds = (active_total + group_size - 1) // group_size

    def build(step_index, cache):
        start = step_index * group_size
        window_ids = lax.dynamic_slice_in_dim(slot_window, start, group_size)
        sim_ids = lax.dynamic_slice_in_dim(slot_sim, start, group_size)
        dots = jnp.einsum(
            "kaf,kbf->kab",
            sim_tiles[sim_ids],
            window[window_ids],
            preferred_element_type=jnp.float32,
        )
        tiles = (
            sim_norm[sim_ids][:, :, None] + real_norm[window_ids][:, None, :] - 2.0 * dots
        ) / features
        return lax.dynamic_update_slice_in_dim(cache, tiles, start, 0)

    cache = lax.fori_loop(0, rounds, build, jnp.zeros((slots, tile_rows, tile_rows), jnp.float32))
    sim_onehot = slot_sim[:, None] == jnp.arange(sim_count)[None, :]
    window_onehot = slot_window[:, None] == jnp.arange(window_count)[None, :]
    mask = alive[:, None, None]

    def gather_stats(scores, axis, onehot, index):
        highest = jnp.max(scores, axis)
        best = jnp.max(jnp.where(onehot[:, :, None], highest[:, None, :], NEG), 0)
        terms = jnp.where(mask, jnp.exp(scores - jnp.expand_dims(best[index], axis)), 0.0)
        partial_value = jnp.sum(terms, axis)
        totals = jnp.dot(
            onehot.T.astype(jnp.float32), partial_value, precision=lax.Precision.HIGHEST
        )
        return (best, totals)

    window_pot = jnp.zeros((window_count, tile_rows), jnp.float32)
    own_pot = jnp.zeros((real_local, tile_rows), jnp.float32)
    sim_pot = jnp.zeros((sim_count, tile_rows), jnp.float32)
    for sweep in range(ITERS):
        row_scores = jnp.where(mask, (window_pot[slot_window][:, None, :] - cache) / EPS, NEG)
        row_best, row_totals = gather_stats(row_scores, 2, sim_onehot, slot_sim)
        sim_pot = -EPS * (row_best + jnp.log(row_totals)) - EPS * log_rows
        column_scores = jnp.where(mask, (sim_pot[slot_sim][:, :, None] - cache) / EPS, NEG)
        column_best, column_totals = gather_stats(column_scores, 1, window_onehot, slot_window)
        column_best, column_totals = joined((column_best, column_totals), "rep", combine)
        column_best = column_best.reshape(3, real_local, tile_rows)
        column_totals = column_totals.reshape(3, real_local, tile_rows)
        upper = guarded(passed_along((column_best[2], column_totals[2]), "blk", 1))
        lower = guarded(passed_along((column_best[0], column_totals[0]), "blk", -1))
        merged = combine(combine((column_best[1], column_totals[1]), upper), lower)
        own = -EPS * (merged[0] + jnp.log(merged[1])) - EPS * log_rows
        beside_all = with_halo(own, (("blk", 0),), real_local)
        own_pot = own
        window_pot = beside_all

    def accumulate(step_index, running):
        sums, totals = running
        start = step_index * group_size
        window_ids = lax.dynamic_slice_in_dim(slot_window, start, group_size)
        sim_ids = lax.dynamic_slice_in_dim(slot_sim, start, group_size)
        flags = lax.dynamic_slice_in_dim(alive, start, group_size)
        tiles = lax.dynamic_slice_in_dim(cache, start, group_size, 0)
        weights = (
            jnp.exp(
                (sim_pot[sim_ids][:, :, None] + window_pot[window_ids][:, None, :] - tiles) / EPS
            )
            * rows_total
        )
        weights = jnp.where(flags[:, None, None], weights, 0.0).astype(jnp.bfloat16)
        products = jnp.einsum(
            "kab,kbf->kaf", weights, window[window_ids], preferred_element_type=jnp.float32
        )
        sums = sums.at[sim_ids].add(products)
        totals = totals.at[sim_ids].add(jnp.sum(weights.astype(jnp.float32), 2))
        return (sums, totals)

    start_sums = jnp.zeros((sim_count, tile_rows, features), jnp.float32)
    start_totals = jnp.zeros((sim_count, tile_rows), jnp.float32)
    sums, totals = lax.fori_loop(0, rounds, accumulate, (start_sums, start_totals))
    pull = totals[:, :, None] * sim_tiles.astype(jnp.float32) - sums
    pull = pull.reshape(sim_count * tile_rows, features)
    sim_out = sim_pot.reshape(-1)
    return (pull, sim_out, own_pot.reshape(-1))


def solution(mesh):
    in_specs = (
        P(("blk", "rep"), None),
        P("blk", "rep"),
        P(("blk", "rep"), None),
        P(("blk", "rep")),
    )
    out_specs = (P(("blk", "rep"), None), P(("blk", "rep")), P("blk"))
    return jax.shard_map(shards, mesh=mesh, in_specs=in_specs, out_specs=out_specs, check_vma=False)
```

profile of v0, /device:TPU:29, one launch (start us, length us, event | category | flops | bytes accessed | tf_op | source)
XLA Modules:
  0.0 454.7 jit_solution(5198647341801647670)
XLA Ops:
  7.9 40.5 %all-gather.8.cloned.1.call-done = bf16[2048,512]{1,0:T(8,128)(2,1)} async-done(((bf16[2048,128]{1,0:T(8,128)(2,1)}), bf16[2048,512]{1,0:T(8,128)(2,1)}) %all-gather.8.cloned.1.call-update) | async-done | bytes 2097168 | tf_op jit(solution)/shard_map/all_gather | solution.py:64
  48.4 4.6 %collective-permute-start = (bf16[2048,512]{1,0:T(8,128)(2,1)}, bf16[2048,512]{1,0:T(8,128)(2,1)S(1)}, u32[]{:S(2)}, u32[]{:S(2)}) collective-permute-start(bf16[2048,512]{1,0:T(8,128)(2,1)} %all-gather.8.cloned.1.call-done), channel_id=1, source_target_pairs={{0,4},{4,8},{8,12},{12,16},{16,20},{20,24},{24,28},{28,32},{32,36}... | collective-permute-start | bytes 6291464 | tf_op jit(solution)/shard_map/ppermute | solution.py:21
  63.6 12.7 %collective-permute-done = bf16[2048,512]{1,0:T(8,128)(2,1)S(1)} collective-permute-done((bf16[2048,512]{1,0:T(8,128)(2,1)}, bf16[2048,512]{1,0:T(8,128)(2,1)S(1)}, u32[]{:S(2)}, u32[]{:S(2)}) %collective-permute-start) | collective-permute-done | bytes 2097184 | tf_op jit(solution)/shard_map/ppermute | solution.py:21
  78.1 7.1 %collective-permute-done.1 = bf16[2048,512]{1,0:T(8,128)(2,1)} collective-permute-done((bf16[2048,512]{1,0:T(8,128)(2,1)}, bf16[2048,512]{1,0:T(8,128)(2,1)}, u32[]{:S(2)}, u32[]{:S(2)}) %collective-permute-start.1) | collective-permute-done | bytes 2097184 | tf_op jit(solution)/shard_map/ppermute | solution.py:24
  87.0 2.7 copy-done.1
  91.0 4.2 broadcast_in_dim.259
  95.2 53.9 %while.58 = (s32[]{:T(128)}, f32[32,256,256]{2,1,0:T(8,128)}, s32[]{:T(128)}, s32[32]{0:T(128)S(1)}, f32[2,256]{1,0:T(2,128)S(1)}, /*index=5*/s32[32]{0:T(128)S(...) while((s32[]{:T(128)}, f32[32,256,256]{2,1,0:T(8,128)}, ...), condition=%wide.region_5.6_spmd, body=%wide.region_4.5_spmd.sunk | while | flops 269486112 | bytes 7373139 | solution.py:100
  95.9 3.4 gather_fusion.1
  102.6 3.4 gather_fusion.1
  109.4 3.4 gather_fusion.1
  116.1 3.4 gather_fusion.1
  122.9 3.4 gather_fusion.1
  129.6 3.4 gather_fusion.1
  136.3 3.4 gather_fusion.1
  143.1 3.4 gather_fusion.1
  149.1 4.7 %fusion.9 = f32[32,256]{1,0:T(8,128)S(1)} fusion(f32[32,256,256]{2,1,0:T(8,128)} %get-tuple-element.646, f32[32,256]{1,0:T(8,128)S(1)} %gather_fusion.9, pred[32]{0:T(512)(128)(4,1)S(1)} %iota_compare_fusion.6), kind=kLoop, calls=%fused_computation.65 | loop fusion | flops 8380416 | bytes 8454176 | tf_op jit(solution)/shard_map/reduce_max | solution.py:106
  154.4 5.4 %select_reduce_fusion.5 = f32[32,256]{1,0:T(8,128)S(1)} fusion(f32[32,256,256]{2,1,0:T(8,128)} %get-tuple-element.646, f32[32,256]{1,0:T(8,128)S(1)} %gather_fusion.10, f32[32,256]{1,0:T(8,128)S(1)} %gather_fusion.9, pred[32]{0:T(512)(128)(4,1)S(1)} %iota_compare_fusion.6), kind=kLoop, calls=%fused_computation.63 | loop fusion | flops 12574720 | bytes 8486944 | tf_op jit(solution)/shard_map/reduce_sum | solution.py:109
  160.5 4.3 fusion.10
  165.6 4.9 %select_reduce_fusion.4 = f32[32,256]{1,0:T(8,128)S(1)} fusion(f32[32,256,256]{2,1,0:T(8,128)} %get-tuple-element.646, f32[32,256]{1,0:T(8,128)S(1)} %gather_fusion.12, f32[32,256]{1,0:T(8,128)S(1)} %gather_fusion.11, pred[32]{0:T(512)(128)(4,1)S(1)} %iota_compare_fusion.6), kind=kLoop, calls=%fused_computation.61 | loop fusion | flops 12574720 | bytes 8486944 | tf_op jit(solution)/shard_map/reduce_sum | solution.py:109
  170.9 7.8 %all-gather.1 = f32[96,256]{1,0:T(8,128)S(1)} all-gather(f32[24,256]{1,0:T(8,128)S(1)} %fusion.26), channel_id=3, replica_groups=mesh['blk'=64,'rep'=4] {'rep'}, dimensions={0}, use_global_device_ids=true | all-gather | bytes 122880 | tf_op jit(solution)/shard_map/all_gather | solution.py:30
  178.7 9.0 %all-gather = f32[96,256]{1,0:T(8,128)S(1)} all-gather(f32[24,256]{1,0:T(8,128)S(1)} %select_reduce_fusion.8), channel_id=2, replica_groups=mesh['blk'=64,'rep'=4] {'rep'}, dimensions={0}, use_global_device_ids=true | all-gather | bytes 122880 | tf_op jit(solution)/shard_map/all_gather | solution.py:30
  191.8 2.4 collective-permute-start.4
  194.2 5.8 %collective-permute-start.5 = (f32[8,256]{1,0:T(8,128)S(1)}, f32[8,256]{1,0:T(8,128)S(1)}, u32[]{:S(2)}, u32[]{:S(2)}) collective-permute-start(f32[8,256]{1,0:T(8,128)S(1)} %get-tuple-element.296), channel_id=1, source_target_pairs={{4,0},{8,4},{12,8},{16,12},{20,16},{24,20},{28,24},{32,28},{36,32}... | collective-permute-start | bytes 24584 | tf_op jit(solution)/shard_map/ppermute | solution.py:40
  202.7 2.6 collective-permute-start.7
  205.4 2.6 collective-permute-done.7
  208.6 4.7 %fusion.11 = f32[32,256]{1,0:T(8,128)S(1)} fusion(f32[32,256,256]{2,1,0:T(8,128)} %get-tuple-element.646, f32[32,256]{1,0:T(8,128)S(1)} %gather_fusion.13, pred[32]{0:T(512)(128)(4,1)S(1)} %iota_compare_fusion.6), kind=kLoop, calls=%fused_computation.67 | loop fusion | flops 8380416 | bytes 8454176 | tf_op jit(solution)/shard_map/reduce_max | solution.py:106
  214.0 5.4 %select_reduce_fusion.3 = f32[32,256]{1,0:T(8,128)S(1)} fusion(f32[32,256,256]{2,1,0:T(8,128)} %get-tuple-element.646, f32[32,256]{1,0:T(8,128)S(1)} %gather_fusion.14, f32[32,256]{1,0:T(8,128)S(1)} %gather_fusion.13, pred[32]{0:T(512)(128)(4,1)S(1)} %iota_compare_fusion.6), kind=kLoop, calls=%fused_computation.59 | loop fusion | flops 12574720 | bytes 8486944 | tf_op jit(solution)/shard_map/reduce_sum | solution.py:109
  220.1 4.3 fusion.12
  225.2 4.9 %select_reduce_fusion.2 = f32[32,256]{1,0:T(8,128)S(1)} fusion(f32[32,256,256]{2,1,0:T(8,128)} %get-tuple-element.646, f32[32,256]{1,0:T(8,128)S(1)} %gather_fusion.16, f32[32,256]{1,0:T(8,128)S(1)} %gather_fusion.15, pred[32]{0:T(512)(128)(4,1)S(1)} %iota_compare_fusion.6), kind=kLoop, calls=%fused_computation.57 | loop fusion | flops 12574720 | bytes 8486944 | tf_op jit(solution)/shard_map/reduce_sum | solution.py:109
  230.4 9.3 %all-gather.3 = f32[96,256]{1,0:T(8,128)S(1)} all-gather(f32[24,256]{1,0:T(8,128)S(1)} %fusion.25), channel_id=5, replica_groups=mesh['blk'=64,'rep'=4] {'rep'}, dimensions={0}, use_global_device_ids=true | all-gather | bytes 122880 | tf_op jit(solution)/shard_map/all_gather | solution.py:30
  239.7 9.2 %all-gather.2 = f32[96,256]{1,0:T(8,128)S(1)} all-gather(f32[24,256]{1,0:T(8,128)S(1)} %select_reduce_fusion.7), channel_id=4, replica_groups=mesh['blk'=64,'rep'=4] {'rep'}, dimensions={0}, use_global_device_ids=true | all-gather | bytes 122880 | tf_op jit(solution)/shard_map/all_gather | solution.py:30
  249.1 9.7 %collective-permute-start.10 = (f32[8,256]{1,0:T(8,128)S(1)}, f32[8,256]{1,0:T(8,128)S(1)}, u32[]{:S(2)}, u32[]{:S(2)}) collective-permute-start(f32[8,256]{1,0:T(8,128)S(1)} %get-tuple-element.294), channel_id=1, source_target_pairs={{4,0},{8,4},{12,8},{16,12},{20,16},{24,20},{28,24},{32,28},{36,32}... | collective-permute-start | bytes 24584 | tf_op jit(solution)/shard_map/ppermute | solution.py:40
  260.7 3.6 collective-permute-start.8
  266.4 1.9 collective-permute-done.9
  268.4 2.9 collective-permute-start.12
  271.3 5.7 %collective-permute-start.13 = (f32[8,256]{1,0:T(8,128)S(1)}, f32[8,256]{1,0:T(8,128)S(1)}, u32[]{:S(2)}, u32[]{:S(2)}) collective-permute-start(f32[8,256]{1,0:T(8,128)S(1)} %multiply_add_fusion.1), channel_id=1, source_target_pairs={{4,0},{8,4},{12,8},{16,12},{20,16},{24,20},{28,24},{32,28},{36,32}... | collective-permute-start | bytes 24584 | tf_op jit(solution)/shard_map/ppermute | solution.py:24
  278.2 4.7 %fusion.13 = f32[32,256]{1,0:T(8,128)S(1)} fusion(f32[32,256,256]{2,1,0:T(8,128)} %get-tuple-element.646, f32[32,256]{1,0:T(8,128)S(1)} %gather_fusion.17, pred[32]{0:T(512)(128)(4,1)S(1)} %iota_compare_fusion.6), kind=kLoop, calls=%fused_computation.69 | loop fusion | flops 8380416 | bytes 8454176 | tf_op jit(solution)/shard_map/reduce_max | solution.py:106
  283.5 5.4 %select_reduce_fusion.1 = f32[32,256]{1,0:T(8,128)S(1)} fusion(f32[32,256,256]{2,1,0:T(8,128)} %get-tuple-element.646, f32[32,256]{1,0:T(8,128)S(1)} %gather_fusion.18, f32[32,256]{1,0:T(8,128)S(1)} %gather_fusion.17, pred[32]{0:T(512)(128)(4,1)S(1)} %iota_compare_fusion.6), kind=kLoop, calls=%fused_computation.55 | loop fusion | flops 12574720 | bytes 8486944 | tf_op jit(solution)/shard_map/reduce_sum | solution.py:109
  289.6 4.3 fusion.14
  294.7 4.9 %select_reduce_fusion = f32[32,256]{1,0:T(8,128)S(1)} fusion(f32[32,256,256]{2,1,0:T(8,128)} %get-tuple-element.646, f32[32,256]{1,0:T(8,128)S(1)} %gather_fusion.20, f32[32,256]{1,0:T(8,128)S(1)} %gather_fusion.19, pred[32]{0:T(512)(128)(4,1)S(1)} %iota_compare_fusion.6), kind=kLoop, calls=%fused_computation.53 | loop fusion | flops 12574720 | bytes 8486944 | tf_op jit(solution)/shard_map/reduce_sum | solution.py:109
  300.0 9.0 %all-gather.5 = f32[96,256]{1,0:T(8,128)S(1)} all-gather(f32[24,256]{1,0:T(8,128)S(1)} %fusion.24), channel_id=7, replica_groups=mesh['blk'=64,'rep'=4] {'rep'}, dimensions={0}, use_global_device_ids=true | all-gather | bytes 122880 | tf_op jit(solution)/shard_map/all_gather | solution.py:30
  309.0 9.0 %all-gather.4 = f32[96,256]{1,0:T(8,128)S(1)} all-gather(f32[24,256]{1,0:T(8,128)S(1)} %select_reduce_fusion.6), channel_id=6, replica_groups=mesh['blk'=64,'rep'=4] {'rep'}, dimensions={0}, use_global_device_ids=true | all-gather | bytes 122880 | tf_op jit(solution)/shard_map/all_gather | solution.py:30
  318.2 6.5 %collective-permute-start.14 = (f32[8,256]{1,0:T(8,128)S(1)}, f32[8,256]{1,0:T(8,128)S(1)}, u32[]{:S(2)}, u32[]{:S(2)}) collective-permute-start(f32[8,256]{1,0:T(8,128)S(1)} %get-tuple-element.289), channel_id=1, source_target_pairs={{0,4},{4,8},{8,12},{12,16},{16,20},{20,24},{24,28},{28,32},{32,36}... | collective-permute-start | bytes 24584 | tf_op jit(solution)/shard_map/ppermute | solution.py:40
  326.7 7.5 %collective-permute-start.16 = (f32[8,256]{1,0:T(8,128)S(1)}, f32[8,256]{1,0:T(8,128)S(1)}, u32[]{:S(2)}, u32[]{:S(2)}) collective-permute-start(f32[8,256]{1,0:T(8,128)S(1)} %get-tuple-element.290), channel_id=1, source_target_pairs={{4,0},{8,4},{12,8},{16,12},{20,16},{24,20},{28,24},{32,28},{36,32}... | collective-permute-start | bytes 24584 | tf_op jit(solution)/shard_map/ppermute | solution.py:40
  334.2 5.8 %collective-permute-start.17 = (f32[8,256]{1,0:T(8,128)S(1)}, f32[8,256]{1,0:T(8,128)S(1)}, u32[]{:S(2)}, u32[]{:S(2)}) collective-permute-start(f32[8,256]{1,0:T(8,128)S(1)} %get-tuple-element.288), channel_id=1, source_target_pairs={{4,0},{8,4},{12,8},{16,12},{20,16},{24,20},{28,24},{32,28},{36,32}... | collective-permute-start | bytes 24584 | tf_op jit(solution)/shard_map/ppermute | solution.py:40
  342.7 2.9 collective-permute-start.19
  348.1 97.5 %while.62 = (s32[]{:T(128)}, f32[2,256,512]{2,1,0:T(8,128)S(1)}, f32[2,256]{1,0:T(2,128)S(1)}, s32[]{:T(128)}, s32[32]{0:T(128)S(1)}, /*index=5*/pred[32]{0:T(51...) while((s32[]{:T(128)}, f32[2,256,512]{2,1,0:T(8,128)S(1)}, ...), condition=%wide.region_34.35_spmd, body=%wide.region_30.34_spmd.sunk | while | flops 271058976 | bytes 13681027 | solution.py:158
  349.5 2.4 convert_reduce_fusion.3
  351.9 4.4 gather_fusion.6
  361.7 2.4 convert_reduce_fusion.3
  364.1 4.4 gather_fusion.6
  373.9 2.4 convert_reduce_fusion.3
  376.3 4.4 gather_fusion.6
  386.1 2.4 convert_reduce_fusion.3
  388.5 4.4 gather_fusion.6
  398.2 2.4 convert_reduce_fusion.3
  400.6 4.4 gather_fusion.6
  410.4 2.4 convert_reduce_fusion.3
  412.8 4.4 gather_fusion.6
  422.6 2.4 convert_reduce_fusion.3
  425.0 4.4 gather_fusion.6
  434.8 2.4 convert_reduce_fusion.3
  437.2 4.4 gather_fusion.6
  445.7 2.2 multiply_subtract_fusion
  (247 shorter events, 112.5 us)
Async XLA Ops:
  7.2 41.2 %all-gather.8.cloned.1.call-start = ((), (), s32[]{:S(2)}) async-start(), calls=%async_computation | async-start | bytes 2621440 | tf_op jit(solution)/shard_map/all_gather | solution.py:64
  48.4 27.9 %collective-permute-start = (bf16[2048,512]{1,0:T(8,128)(2,1)}, bf16[2048,512]{1,0:T(8,128)(2,1)S(1)}, u32[]{:S(2)}, u32[]{:S(2)}) collective-permute-start(bf16[2048,512]{1,0:T(8,128)(2,1)} %all-gather.8.cloned.1.call-done), channel_id=1, source_target_pairs={{0,4},{4,8},{8,12},{12,16},{16,20},{20,24},{24,28},{28,32},{32,36}... | collective-permute-start | bytes 6291464 | tf_op jit(solution)/shard_map/ppermute | solution.py:21
  57.6 27.7 %collective-permute-start.1 = (bf16[2048,512]{1,0:T(8,128)(2,1)}, bf16[2048,512]{1,0:T(8,128)(2,1)}, u32[]{:S(2)}, u32[]{:S(2)}) collective-permute-start(bf16[2048,512]{1,0:T(8,128)(2,1)} %all-gather.8.cloned.1.call-done), channel_id=1, source_target_pairs={{4,0},{8,4},{12,8},{16,12},{20,16},{24,20},{28,24},{32,28},{36,32}... | collective-permute-start | bytes 6291464 | tf_op jit(solution)/shard_map/ppermute | solution.py:24
  86.9 2.7 copy-start.1
  89.7 5.5 %copy-start = (bf16[512,512]{1,0:T(8,128)(2,1)S(1)}, bf16[512,512]{1,0:T(8,128)(2,1)}, u32[]{:S(2)}) copy-start(bf16[512,512]{1,0:T(8,128)(2,1)} %param.14) | copy-start | bytes 1572868
  187.9 12.0 %collective-permute-start.2 = (f32[8,256]{1,0:T(8,128)S(1)}, f32[8,256]{1,0:T(8,128)S(1)}, u32[]{:S(2)}, u32[]{:S(2)}) collective-permute-start(f32[8,256]{1,0:T(8,128)S(1)} %get-tuple-element.297), channel_id=1, source_target_pairs={{0,4},{4,8},{8,12},{12,16},{16,20},{20,24},{24,28},{28,32},{32,36}... | collective-permute-start | bytes 24584 | tf_op jit(solution)/shard_map/ppermute | solution.py:40
  189.9 10.1 %collective-permute-start.3 = (f32[8,256]{1,0:T(8,128)S(1)}, f32[8,256]{1,0:T(8,128)S(1)}, u32[]{:S(2)}, u32[]{:S(2)}) collective-permute-start(f32[8,256]{1,0:T(8,128)S(1)} %get-tuple-element.295), channel_id=1, source_target_pairs={{0,4},{4,8},{8,12},{12,16},{16,20},{20,24},{24,28},{28,32},{32,36}... | collective-permute-start | bytes 24584 | tf_op jit(solution)/shard_map/ppermute | solution.py:40
  191.8 8.2 %collective-permute-start.4 = (f32[8,256]{1,0:T(8,128)S(1)}, f32[8,256]{1,0:T(8,128)S(1)}, u32[]{:S(2)}, u32[]{:S(2)}) collective-permute-start(f32[8,256]{1,0:T(8,128)S(1)} %get-tuple-element.298), channel_id=1, source_target_pairs={{4,0},{8,4},{12,8},{16,12},{20,16},{24,20},{28,24},{32,28},{36,32}... | collective-permute-start | bytes 24584 | tf_op jit(solution)/shard_map/ppermute | solution.py:40
  194.2 6.6 %collective-permute-start.5 = (f32[8,256]{1,0:T(8,128)S(1)}, f32[8,256]{1,0:T(8,128)S(1)}, u32[]{:S(2)}, u32[]{:S(2)}) collective-permute-start(f32[8,256]{1,0:T(8,128)S(1)} %get-tuple-element.296), channel_id=1, source_target_pairs={{4,0},{8,4},{12,8},{16,12},{20,16},{24,20},{28,24},{32,28},{36,32}... | collective-permute-start | bytes 24584 | tf_op jit(solution)/shard_map/ppermute | solution.py:40
  200.8 4.6 %collective-permute-start.6 = (f32[8,256]{1,0:T(8,128)S(1)}, f32[8,256]{1,0:T(8,128)S(1)}, u32[]{:S(2)}, u32[]{:S(2)}) collective-permute-start(f32[8,256]{1,0:T(8,128)S(1)} %multiply_add_fusion.2), channel_id=1, source_target_pairs={{0,4},{4,8},{8,12},{12,16},{16,20},{20,24},{24,28},{28,32},{32,36}... | collective-permute-start | bytes 24584 | tf_op jit(solution)/shard_map/ppermute | solution.py:21
  202.7 5.3 %collective-permute-start.7 = (f32[8,256]{1,0:T(8,128)S(1)}, f32[8,256]{1,0:T(8,128)S(1)}, u32[]{:S(2)}, u32[]{:S(2)}) collective-permute-start(f32[8,256]{1,0:T(8,128)S(1)} %multiply_add_fusion.2), channel_id=1, source_target_pairs={{4,0},{8,4},{12,8},{16,12},{20,16},{24,20},{28,24},{32,28},{36,32}... | collective-permute-start | bytes 24584 | tf_op jit(solution)/shard_map/ppermute | solution.py:24
  249.1 17.2 %collective-permute-start.10 = (f32[8,256]{1,0:T(8,128)S(1)}, f32[8,256]{1,0:T(8,128)S(1)}, u32[]{:S(2)}, u32[]{:S(2)}) collective-permute-start(f32[8,256]{1,0:T(8,128)S(1)} %get-tuple-element.294), channel_id=1, source_target_pairs={{4,0},{8,4},{12,8},{16,12},{20,16},{24,20},{28,24},{32,28},{36,32}... | collective-permute-start | bytes 24584 | tf_op jit(solution)/shard_map/ppermute | solution.py:40
  258.8 7.5 %collective-permute-start.11 = (f32[8,256]{1,0:T(8,128)S(1)}, f32[8,256]{1,0:T(8,128)S(1)}, u32[]{:S(2)}, u32[]{:S(2)}) collective-permute-start(f32[8,256]{1,0:T(8,128)S(1)} %get-tuple-element.292), channel_id=1, source_target_pairs={{4,0},{8,4},{12,8},{16,12},{20,16},{24,20},{28,24},{32,28},{36,32}... | collective-permute-start | bytes 24584 | tf_op jit(solution)/shard_map/ppermute | solution.py:40
  260.7 5.7 %collective-permute-start.8 = (f32[8,256]{1,0:T(8,128)S(1)}, f32[8,256]{1,0:T(8,128)S(1)}, u32[]{:S(2)}, u32[]{:S(2)}) collective-permute-start(f32[8,256]{1,0:T(8,128)S(1)} %get-tuple-element.293), channel_id=1, source_target_pairs={{0,4},{4,8},{8,12},{12,16},{16,20},{20,24},{24,28},{28,32},{32,36}... | collective-permute-start | bytes 24584 | tf_op jit(solution)/shard_map/ppermute | solution.py:40
  264.4 4.0 collective-permute-start.9
  268.4 8.6 %collective-permute-start.12 = (f32[8,256]{1,0:T(8,128)S(1)}, f32[8,256]{1,0:T(8,128)S(1)}, u32[]{:S(2)}, u32[]{:S(2)}) collective-permute-start(f32[8,256]{1,0:T(8,128)S(1)} %multiply_add_fusion.1), channel_id=1, source_target_pairs={{0,4},{4,8},{8,12},{12,16},{16,20},{20,24},{24,28},{28,32},{32,36}... | collective-permute-start | bytes 24584 | tf_op jit(solution)/shard_map/ppermute | solution.py:21
  271.3 6.2 %collective-permute-start.13 = (f32[8,256]{1,0:T(8,128)S(1)}, f32[8,256]{1,0:T(8,128)S(1)}, u32[]{:S(2)}, u32[]{:S(2)}) collective-permute-start(f32[8,256]{1,0:T(8,128)S(1)} %multiply_add_fusion.1), channel_id=1, source_target_pairs={{4,0},{8,4},{12,8},{16,12},{20,16},{24,20},{28,24},{32,28},{36,32}... | collective-permute-start | bytes 24584 | tf_op jit(solution)/shard_map/ppermute | solution.py:24
  318.2 21.7 %collective-permute-start.14 = (f32[8,256]{1,0:T(8,128)S(1)}, f32[8,256]{1,0:T(8,128)S(1)}, u32[]{:S(2)}, u32[]{:S(2)}) collective-permute-start(f32[8,256]{1,0:T(8,128)S(1)} %get-tuple-element.289), channel_id=1, source_target_pairs={{0,4},{4,8},{8,12},{12,16},{16,20},{20,24},{24,28},{28,32},{32,36}... | collective-permute-start | bytes 24584 | tf_op jit(solution)/shard_map/ppermute | solution.py:40
  324.8 15.2 %collective-permute-start.15 = (f32[8,256]{1,0:T(8,128)S(1)}, f32[8,256]{1,0:T(8,128)S(1)}, u32[]{:S(2)}, u32[]{:S(2)}) collective-permute-start(f32[8,256]{1,0:T(8,128)S(1)} %get-tuple-element.287), channel_id=1, source_target_pairs={{0,4},{4,8},{8,12},{12,16},{16,20},{20,24},{24,28},{28,32},{32,36}... | collective-permute-start | bytes 24584 | tf_op jit(solution)/shard_map/ppermute | solution.py:40
  326.7 13.3 %collective-permute-start.16 = (f32[8,256]{1,0:T(8,128)S(1)}, f32[8,256]{1,0:T(8,128)S(1)}, u32[]{:S(2)}, u32[]{:S(2)}) collective-permute-start(f32[8,256]{1,0:T(8,128)S(1)} %get-tuple-element.290), channel_id=1, source_target_pairs={{4,0},{8,4},{12,8},{16,12},{20,16},{24,20},{28,24},{32,28},{36,32}... | collective-permute-start | bytes 24584 | tf_op jit(solution)/shard_map/ppermute | solution.py:40
  334.2 6.6 %collective-permute-start.17 = (f32[8,256]{1,0:T(8,128)S(1)}, f32[8,256]{1,0:T(8,128)S(1)}, u32[]{:S(2)}, u32[]{:S(2)}) collective-permute-start(f32[8,256]{1,0:T(8,128)S(1)} %get-tuple-element.288), channel_id=1, source_target_pairs={{4,0},{8,4},{12,8},{16,12},{20,16},{24,20},{28,24},{32,28},{36,32}... | collective-permute-start | bytes 24584 | tf_op jit(solution)/shard_map/ppermute | solution.py:40
  340.8 6.1 %collective-permute-start.18 = (f32[8,256]{1,0:T(8,128)S(1)}, f32[8,256]{1,0:T(8,128)S(1)}, u32[]{:S(2)}, u32[]{:S(2)}) collective-permute-start(f32[8,256]{1,0:T(8,128)S(1)} %multiply_add_fusion), channel_id=1, source_target_pairs={{0,4},{4,8},{8,12},{12,16},{16,20},{20,24},{24,28},{28,32},{32,36}... | collective-permute-start | bytes 24584 | tf_op jit(solution)/shard_map/ppermute | solution.py:21
  342.7 5.3 %collective-permute-start.19 = (f32[8,256]{1,0:T(8,128)S(1)}, f32[8,256]{1,0:T(8,128)S(1)}, u32[]{:S(2)}, u32[]{:S(2)}) collective-permute-start(f32[8,256]{1,0:T(8,128)S(1)} %multiply_add_fusion), channel_id=1, source_target_pairs={{4,0},{8,4},{12,8},{16,12},{20,16},{24,20},{28,24},{32,28},{36,32}... | collective-permute-start | bytes 24584 | tf_op jit(solution)/shard_map/ppermute | solution.py:24
Sparse Core Ops, SparseCore 0:
  9.8 38.5 all-gather.7
where the time goes:
time: 457 us; the launch traced here: 455 us
  other arithmetic  107 us (23%)
  local copies, waits for them, and re-layouts  106 us (23%)
  starting transfers between devices  75.4 us (16%)
  waiting for transfers between devices  68.9 us (15%)
  blocking collectives  53.4 us (12%)
  matrix products  27.6 us (6%)
  between operations  15.4 us (3%)
    all_gather x6, blocking collectives, joined(): pieces = jax.tree.map(lambda part: lax.all_gather(part, axis), value)  53.4 us
    ppermute x12, starting transfers between devices, passed_along(): return lax.ppermute(value, axis, pairs)  50.9 us
    all_gather x1, waiting for transfers between devices, shards(): whole = lax.all_gather(real, 'rep', axis=1, tiled=True)  40.5 us
    gather x8, local copies, waits for them, and re-layouts, accumulate(): window[window_ids]  34.9 us
    reduce_sum x6, other arithmetic, gather_stats(): partial_value = jnp.sum(terms, axis)  30.9 us
    gather x8, local copies, waits for them, and re-layouts, build(): window[window_ids]  27.2 us
    reduce_max x6, other arithmetic, gather_stats(): highest = jnp.max(scores, axis)  26.9 us
    reduce_sum x8, other arithmetic, accumulate(): totals = totals.at[sim_ids].add(jnp.sum(weights.astype(jnp.float32), 2))  19.2 us
  transfers between devices with their start and end apart: 21, of which 10 were waited for; matrix products, arithmetic and copies ran while one was open for 2% of the time, Pallas kernels for 0%

commit v1 on v0

v1 whole, which is shorter than its diff:
```python
import functools
import math

import jax
import jax.numpy as jnp
from jax import lax
from jax.experimental import pallas as pl
from jax.experimental.pallas import tpu as pltpu
from jax.sharding import PartitionSpec as P

BLOCK = 256
ITERS = 3
EPS = 0.05
NEG = -1e30
LOG2E = math.log2(math.e)
LANES = 128
MIB = 1024 * 1024


def log_add(a, b):
    high = jnp.maximum(a, b)
    return high + jnp.log2(jnp.exp2(a - high) + jnp.exp2(b - high))


def core_swap(value):
    owners = lax.axis_size("blk")
    return lax.ppermute(value, "blk", [(i, i ^ 1) for i in range(owners)])


def chip_swap(value):
    owners = lax.axis_size("blk")
    return lax.ppermute(value, "blk", [(i, (((i + 1) ^ 1) - 1) % owners) for i in range(owners)])


def rep_shift(value, by):
    count = lax.axis_size("rep")
    return lax.ppermute(value, "rep", [(i, (i + by) % count) for i in range(count)])


def rep_flip(value, mask):
    count = lax.axis_size("rep")
    return lax.ppermute(value, "rep", [(i, i ^ mask) for i in range(count)])


def row_pass(cnt_ref, tab_ref, g_ref, vh_ref, u_ref, log_rows):
    part = 128
    for e in range(2):
        count = cnt_ref[e]
        for c in range(BLOCK // part):
            rows = slice(c * part, (c + 1) * part)

            def scores(k):
                vrow = vh_ref[pl.ds(tab_ref[e, k], 1), :]
                return g_ref[e * 16 + k, rows, :] + vrow

            def peak(k, high):
                t = scores(k)
                return jnp.maximum(high, jnp.maximum(t[:, :LANES], t[:, LANES:]))

            high = lax.fori_loop(0, count, peak, jnp.full((part, LANES), NEG, jnp.float32))
            high = jnp.broadcast_to(jnp.max(high, axis=1, keepdims=True), (part, LANES))

            def total(k, acc):
                t = scores(k)
                return acc + jnp.exp2(t[:, :LANES] - high) + jnp.exp2(t[:, LANES:] - high)

            acc = lax.fori_loop(0, count, total, jnp.zeros((part, LANES), jnp.float32))
            acc = jnp.broadcast_to(jnp.sum(acc, axis=1, keepdims=True), (part, LANES))
            u_ref[e * BLOCK + c * part : e * BLOCK + (c + 1) * part, :] = (
                -(high + jnp.log2(acc)) - log_rows
            )


def column_pass(cnt_ref, tab_ref, g_ref, u_ref, l_ref):
    window = l_ref.shape[0]
    row_ids = lax.broadcasted_iota(jnp.int32, (window, LANES), 0)
    stats = []
    for e in range(2):

        def tile(k, carry):
            here = row_ids == tab_ref[e, k]
            after = []
            for half in range(2):
                lanes = slice(half * LANES, (half + 1) * LANES)
                highs, sums = carry[half]
                t = g_ref[e * 16 + k, :, lanes] + u_ref[e * BLOCK : (e + 1) * BLOCK, :]
                high = jnp.max(t, axis=0, keepdims=True)
                total = jnp.sum(jnp.exp2(t - high), axis=0, keepdims=True)
                after.append((jnp.where(here, high, highs), jnp.where(here, total, sums)))
            return tuple(after)

        start = (jnp.full((window, LANES), NEG, jnp.float32), jnp.ones((window, LANES), jnp.float32))
        found = lax.fori_loop(0, cnt_ref[e], tile, (start, start))
        stats.append([high + jnp.log2(total) for high, total in found])
    for half in range(2):
        l_ref[:, half * LANES : (half + 1) * LANES] = log_add(stats[0][half], stats[1][half])


def build_kernel(
    log_rows, scale, cnt_ref, tab_ref, q_ref, sim_ref, vh_ref, *refs
):
    pieces, (g_ref, win_ref, l_ref), scratch = refs[:12], refs[12:15], refs[15:]
    u_ref, sems = scratch
    rows = pieces[0].shape[0]
    copies = []
    for group in range(3):
        for source in range(4):
            q = pl.multiple_of(q_ref[source] * LANES, LANES)
            i = group * 4 + source
            copies.append(
                pltpu.make_async_copy(
                    pieces[i],
                    win_ref.at[pl.ds(group * rows, rows), pl.ds(q, LANES)],
                    sems.at[i],
                )
            )
    for copy in copies:
        copy.start()
    for copy in copies:
        copy.wait()
    for e in range(2):

        def tile(k, carry):
            w = tab_ref[e, k]
            start = pl.multiple_of(w * BLOCK, BLOCK)
            dots = lax.dot_general(
                sim_ref[e * BLOCK : (e + 1) * BLOCK, :],
                win_ref[pl.ds(start, BLOCK), :],
                (((1,), (1,)), ((), ())),
                preferred_element_type=jnp.float32,
            )
            g_ref[e * 16 + k] = dots * scale
            return carry

        lax.fori_loop(0, cnt_ref[e], tile, 0)
    row_pass(cnt_ref, tab_ref, g_ref, vh_ref, u_ref, log_rows)
    column_pass(cnt_ref, tab_ref, g_ref, u_ref, l_ref)


def sweep_kernel(log_rows, cnt_ref, tab_ref, v0_ref, v1_ref, v2_ref, g_ref, l_ref, u_ref, row_ref, vh_ref):
    local = v0_ref.shape[0]
    vh_ref[0:local, :] = v0_ref[...]
    vh_ref[local : 2 * local, :] = v1_ref[...]
    vh_ref[2 * local : 3 * local, :] = v2_ref[...]
    row_pass(cnt_ref, tab_ref, g_ref, vh_ref, u_ref, log_rows)
    for e in range(2):
        row_ref[e : e + 1, :] = jnp.transpose(u_ref[e * BLOCK : (e + 1) * BLOCK, :])[0:1, :]
    column_pass(cnt_ref, tab_ref, g_ref, u_ref, l_ref)


def pull_kernel(log_rows, cnt_ref, tab_ref, v0_ref, v1_ref, v2_ref, u_ref, sim_ref, g_ref, win_ref, out_ref, vh_ref, tot_ref):
    local = v0_ref.shape[0]
    vh_ref[0:local, :] = v0_ref[...]
    vh_ref[local : 2 * local, :] = v1_ref[...]
    vh_ref[2 * local : 3 * local, :] = v2_ref[...]
    for e in range(2):
        rows = slice(e * BLOCK, (e + 1) * BLOCK)
        out_ref[rows, :] = jnp.zeros((BLOCK, out_ref.shape[1]), jnp.float32)
        tot_ref[...] = jnp.zeros(tot_ref.shape, jnp.float32)

        def tile(k, carry):
            w = tab_ref[e, k]
            vrow = vh_ref[pl.ds(w, 1), :] + log_rows
            u = u_ref[rows, :]
            t = g_ref[e * 16 + k]
            left = jnp.exp2(t[:, :LANES] + u + vrow[:, :LANES]).astype(jnp.bfloat16)
            right = jnp.exp2(t[:, LANES:] + u + vrow[:, LANES:]).astype(jnp.bfloat16)
            tot_ref[...] += left.astype(jnp.float32) + right.astype(jnp.float32)
            start = pl.multiple_of(w * BLOCK, BLOCK)
            out_ref[rows, :] += jnp.dot(
                jnp.concatenate([left, right], axis=1),
                win_ref[pl.ds(start, BLOCK), :],
                preferred_element_type=jnp.float32,
            )
            return carry

        lax.fori_loop(0, cnt_ref[e], tile, 0)
        totals = jnp.sum(tot_ref[...], axis=1, keepdims=True)
        out_ref[rows, :] = totals * sim_ref[rows, :].astype(jnp.float32) - out_ref[rows, :]


def vmem():
    return pl.BlockSpec(memory_space=pltpu.VMEM)


def smem():
    return pl.BlockSpec(memory_space=pltpu.SMEM)


def shards(sim, real, pair_real, pair_count):
    replicas = lax.axis_size("rep")
    owners = lax.axis_size("blk")
    features = sim.shape[1]
    local = real.shape[0] // BLOCK
    rows_total = owners * real.shape[0]
    log_rows = math.log2(rows_total)
    unit = LOG2E / EPS / features
    mine = lax.axis_index("blk")
    rep = lax.axis_index("rep")
    fan = pair_real.shape[1]
    group = pair_real // local - mine
    group = jnp.clip(jnp.where(mine % 2 == 0, group + 1, 1 - group), 0, 2)
    table = group * local + pair_real % local
    quarters = (rep + jnp.array([0, replicas - 1, 1, 2], jnp.int32)) % replicas

    own = real
    from_low = rep_shift(own, 1)
    from_high = rep_shift(own, -1)
    half = own.shape[0] // 2
    far_a = rep_shift(from_low[:half], 1)
    far_b = rep_shift(from_high[half:], -1)
    near = jnp.stack([from_low, from_high])
    far = jnp.concatenate([far_a, far_b])
    pieces = []
    middle = [own, from_low, from_high, far]
    sides = []
    for swap in (chip_swap, core_swap):
        first = swap(own)
        second = swap(near)
        third = swap(far)
        sides.append([first, second[0], second[1], third])
    groups = [sides[0], middle, sides[1]]
    pieces = [piece for parts in groups for piece in parts]
    norms = [
        sum(jnp.sum(jnp.square(p.astype(jnp.float32)), -1) for p in parts).reshape(local, BLOCK) * unit
        for parts in groups
    ]
    sim_norm = jnp.sum(jnp.square(sim.astype(jnp.float32)), -1) * unit

    tiles = 2 * fan
    window = 3 * local
    stats_shape = jax.ShapeDtypeStruct((window, BLOCK), jnp.float32)
    potentials = pltpu.VMEM((2 * BLOCK, LANES), jnp.float32)
    cost, window_rows, stats_out = pl.pallas_call(
        functools.partial(build_kernel, log_rows, 2.0 * unit),
        out_shape=[
            pltpu.VMEM((tiles, BLOCK, BLOCK), jnp.float32),
            pltpu.VMEM((window * BLOCK, features), jnp.bfloat16),
            stats_shape,
        ],
        in_specs=[smem()] * 3 + [vmem()] * 2 + [pl.BlockSpec(memory_space=pl.ANY)] * 12,
        out_specs=[vmem()] * 3,
        scratch_shapes=[potentials, pltpu.SemaphoreType.DMA((12,))],
        compiler_params=pltpu.CompilerParams(vmem_limit_bytes=30 * MIB),
    )(pair_count, table, quarters, sim, -jnp.concatenate(norms), *pieces)

    for sweep in range(ITERS):
        if sweep:
            stats_out, sim_pot, sim_row = pl.pallas_call(
                functools.partial(sweep_kernel, log_rows),
                out_shape=[
                    stats_shape,
                    jax.ShapeDtypeStruct((2 * BLOCK, LANES), jnp.float32),
                    jax.ShapeDtypeStruct((2, BLOCK), jnp.float32),
                ],
                in_specs=[smem()] * 2 + [vmem()] * 4,
                out_specs=[vmem()] * 3,
                scratch_shapes=[pltpu.VMEM((window, BLOCK), jnp.float32)],
                compiler_params=pltpu.CompilerParams(vmem_limit_bytes=30 * MIB),
            )(pair_count, table, *around, pltpu.with_memory_space_constraint(cost, pltpu.VMEM))
        merged = log_add(stats_out, rep_flip(stats_out, 1))
        merged = log_add(merged, rep_flip(merged, 3))
        from_core = core_swap(merged[2 * local :])
        from_chip = chip_swap(merged[:local])
        potential = -log_add(log_add(merged[local : 2 * local], from_core), from_chip) - log_rows
        around = (chip_swap(potential), potential, core_swap(potential))

    pull = pl.pallas_call(
        functools.partial(pull_kernel, log_rows),
        out_shape=jax.ShapeDtypeStruct(sim.shape, jnp.float32),
        in_specs=[smem()] * 2 + [vmem()] * 7,
        out_specs=vmem(),
        scratch_shapes=[
            pltpu.VMEM((window, BLOCK), jnp.float32),
            pltpu.VMEM((BLOCK, LANES), jnp.float32),
        ],
        compiler_params=pltpu.CompilerParams(vmem_limit_bytes=30 * MIB),
    )(
        pair_count,
        table,
        *around,
        sim_pot,
        sim,
        pltpu.with_memory_space_constraint(cost, pltpu.VMEM),
        pltpu.with_memory_space_constraint(window_rows, pltpu.VMEM),
    )
    back = EPS / LOG2E
    sim_out = (sim_row.reshape(-1) + sim_norm) * back
    real_out = ((potential + norms[1]) * back).reshape(-1)
    return (pull, sim_out, real_out)


def solution(mesh):
    in_specs = (
        P(("blk", "rep"), None),
        P("blk", "rep"),
        P(("blk", "rep"), None),
        P(("blk", "rep")),
    )
    out_specs = (P(("blk", "rep"), None), P(("blk", "rep")), P("blk"))
    return jax.shard_map(shards, mesh=mesh, in_specs=in_specs, out_specs=out_specs, check_vma=False)
```

time: 457 us -> 149 us (0.33)
  the two profiles are of different devices: /device:TPU:29 before, /device:TPU:0 now
where the time goes in v1:
time: 149 us; the launch traced here: 151 us
  waiting for transfers between devices  74.4 us (50%)
  Pallas kernels  31.9 us (21%)
  starting transfers between devices  26.2 us (18%)
  other arithmetic  14.1 us (9%)
  local copies, waits for them, and re-layouts  3.28 us (2%)
    ppermute x9, waiting for transfers between devices, chip_swap(): lax.ppermute(value, 'blk', [(i, ((i + 1 ^ 1) - 1) % owners) for i in rang...  43.4 us
    ppermute x6, waiting for transfers between devices, rep_flip(): return lax.ppermute(value, 'rep', [(i, i ^ mask) for i in range(count)])  26.5 us
    ppermute x9, starting transfers between devices, chip_swap(): lax.ppermute(value, 'blk', [(i, ((i + 1 ^ 1) - 1) % owners) for i in rang...  18.4 us
    pallas_call x1, Pallas kernels, shards(): pl.pallas_call(functools.partial(build_kernel, log_rows, 2.0 * unit), out...  13.4 us
    pallas_call x2, Pallas kernels, shards(): pl.pallas_call(functools.partial(sweep_kernel, log_rows), out_shape=[stat...  11.6 us
    reduce_sum x10, other arithmetic, shards(): jnp.sum(jnp.square(p.astype(jnp.float32)), -1)  10.6 us
    pallas_call x1, Pallas kernels, shards(): pl.pallas_call(functools.partial(pull_kernel, log_rows), out_shape=jax.Sh...  6.95 us
    ppermute x4, starting transfers between devices, rep_shift(): lax.ppermute(value, 'rep', [(i, (i + by) % count) for i in range(count)])  6.7 us
  transfers between devices with their start and end apart: 28, of which 17 were waited for; matrix products, arithmetic and copies ran while one was open for 8% of the time, Pallas kernels for 0%

profile of v1, /device:TPU:0, one launch (start us, length us, event | category | flops | bytes accessed | tf_op | source)
XLA Modules:
  0.0 151.0 jit_solution(12465488291793347122)
XLA Ops:
  0.7 0.1 collective-permute-start.1
  0.8 3.2 %collective-permute-start.2 = (bf16[2048,128]{1,0:T(8,128)(2,1)}, bf16[2048,128]{1,0:T(8,128)(2,1)S(1)}, u32[]{:S(2)}, u32[]{:S(2)}) collective-permute-start(bf16[2048,128]{1,0:T(8,128)(2,1)} %refs_4_.1), channel_id=1, source_target_pairs={{0,3},{1,0},{2,1},{3,2},{4,7},{5,4},{6,5},{7,6},{8,11},{9,8},{10,9... | collective-permute-start | bytes 1572872 | tf_op jit(solution)/shard_map/ppermute | solution.py:37
  4.0 5.4 %collective-permute-start = (bf16[2048,128]{1,0:T(8,128)(2,1)}, bf16[2048,128]{1,0:T(8,128)(2,1)S(1)}, u32[]{:S(2)}, u32[]{:S(2)}) collective-permute-start(bf16[2048,128]{1,0:T(8,128)(2,1)} %refs_4_.1), channel_id=1, source_target_pairs={{0,252},{4,8},{8,4},{12,16},{16,12},{20,24},{24,20},{28,32},{32,28... | collective-permute-start | bytes 1572872 | tf_op jit(solution)/shard_map/ppermute | solution.py:32
  9.4 1.4 multiply_reduce_fusion.8
  10.8 0.7 and_select_fusion.q_ref
  11.5 0.7 fusion.24.tab_ref
  12.2 1.7 %collective-permute-done.1.refs_5_ = bf16[2048,128]{1,0:T(8,128)(2,1)S(1)} collective-permute-done((bf16[2048,128]{1,0:T(8,128)(2,1)}, bf16[2048,128]{1,0:T(8,128)(2,1)S(1)}, u32[]{:S(2)}, u32[]{:S(2)}) %collective-permute-start.1) | collective-permute-done | bytes 524320 | tf_op jit(solution)/shard_map/ppermute | solution.py:37
  13.9 0.6 collective-permute-start.4
  14.5 2.8 %collective-permute-start.5 = (bf16[1024,128]{1,0:T(8,128)(2,1)S(1)}, bf16[1024,128]{1,0:T(8,128)(2,1)S(1)}, u32[]{:S(2)}, u32[]{:S(2)}) collective-permute-start(bf16[1024,128]{1,0:T(8,128)(2,1)S(1)} %slice.63), channel_id=1, source_target_pairs={{0,3},{1,0},{2,1},{3,2},{4,7},{5,4},{6,5},{7,6},{8,11},{9,8},{10,9... | collective-permute-start | bytes 786440 | tf_op jit(solution)/shard_map/ppermute | solution.py:37
  17.3 1.1 pad_maximum_fusion
  18.4 6.5 %collective-permute-start.3 = (bf16[2,2048,128]{2,1,0:T(8,128)(2,1)}, bf16[2,2048,128]{2,1,0:T(8,128)(2,1)}, u32[]{:S(2)}, u32[]{:S(2)}) collective-permute-start(bf16[2,2048,128]{2,1,0:T(8,128)(2,1)} %pad_maximum_fusion), channel_id=1, source_target_pairs={{0,252},{4,8},{8,4},{12,16},{16,12},{20,24},{24,20},{28,32},{32,28... | collective-permute-start | bytes 3145736 | tf_op jit(solution)/shard_map/ppermute | solution.py:32
  24.9 0.3 multiply_reduce_fusion.6
  25.2 0.3 multiply_reduce_fusion.7
  25.6 0.1 collective-permute-start.8
  25.8 5.4 %collective-permute-start.6 = (bf16[2048,128]{1,0:T(8,128)(2,1)S(1)}, bf16[2048,128]{1,0:T(8,128)(2,1)}, u32[]{:S(2)}, u32[]{:S(2)}) collective-permute-start(bf16[2048,128]{1,0:T(8,128)(2,1)S(1)} %constant_dynamic-update-slice_fusion.refs_7_), channel_id=1, source_target_pairs={{0,252},{4,8},{8,4},{12,16},{16,12},{20,24},{24,20},{28,32},{32,28... | collective-permute-start | bytes 1572872 | tf_op jit(solution)/shard_map/ppermute | solution.py:32
  31.2 0.3 multiply_reduce_fusion.12
  31.5 0.1 collective-permute-start.9
  31.6 1.4 multiply_reduce_fusion.4
  33.0 0.3 multiply_reduce_fusion.5
  33.4 9.9 %collective-permute-done.6.refs_3_ = bf16[2048,128]{1,0:T(8,128)(2,1)} collective-permute-done((bf16[2048,128]{1,0:T(8,128)(2,1)S(1)}, bf16[2048,128]{1,0:T(8,128)(2,1)}, u32[]{:S(2)}, u32[]{:S(2)}) %collective-permute-start.6) | collective-permute-done | bytes 524320 | tf_op jit(solution)/shard_map/ppermute | solution.py:32
  43.3 1.4 multiply_reduce_fusion.9
  44.7 1.4 multiply_reduce_fusion.1
  46.1 1.8 %multiply_reduce_fusion.11 = (f32[2048]{0:T(1024)S(1)}, f32[2048]{0:T(1024)S(1)}) fusion(bf16[2,2048,128]{2,1,0:T(8,128)(2,1)} %collective-permute-done.3), kind=kLoop, calls=%fused_computation.12 | loop fusion | flops 1568768 | bytes 1064960 | tf_op jit(solution)/shard_map/reduce_sum | solution.py:225
  48.0 1.8 %multiply_reduce_fusion.3 = (f32[2048]{0:T(1024)S(1)}, f32[2048]{0:T(1024)S(1)}) fusion(bf16[2,2048,128]{2,1,0:T(8,128)(2,1)} %collective-permute-done.8), kind=kLoop, calls=%fused_computation.4 | loop fusion | flops 1568768 | bytes 1064960 | tf_op jit(solution)/shard_map/reduce_sum | solution.py:225
  49.8 1.3 slice_bitcast_fusion
  51.1 1.3 slice_bitcast_fusion.2
  52.4 13.4 %shard_map.76 = (f32[32,256,256]{2,1,0:T(8,128)S(1)}, bf16[6144,512]{1,0:T(8,128)(2,1)S(1)}, f32[24,256]{1,0:T(8,128)S(1)}) custom-call(s32[2]{0:T(128)S(1)} %copy-done.2, s32[2,16]{1,0:T(2,128)S(1)} %fusion.24.tab_ref, s32[4]{0:T(128)S(1)} %and_select_fusion.q_ref, bf16[512,512]{1,0:T(8,128)(2,1)S(1)} %copy-done, f32[24,256]{1,0:T(8,128)S(1)} %maximum_negate_fusion.vh_ref, ...), custom_call_target="tpu_custom_call" | custom-call | tf_op jit(solution)/shard_map/pallas_call | solution.py:234
  65.8 0.1 collective-permute-start.10
  65.9 3.8 %collective-permute-done.10 = f32[24,256]{1,0:T(8,128)S(1)} collective-permute-done((f32[24,256]{1,0:T(8,128)S(1)}, f32[24,256]{1,0:T(8,128)S(1)}, u32[]{:S(2)}, u32[]{:S(2)}) %collective-permute-start.10) | collective-permute-done | bytes 24608 | tf_op jit(solution)/shard_map/ppermute | solution.py:42
  69.8 0.1 collective-permute-start.11
  69.9 5.0 %collective-permute-done.11 = f32[24,256]{1,0:T(8,128)S(1)} collective-permute-done((f32[24,256]{1,0:T(8,128)S(1)}, f32[24,256]{1,0:T(8,128)S(1)}, u32[]{:S(2)}, u32[]{:S(2)}) %collective-permute-start.11) | collective-permute-done | bytes 24608 | tf_op jit(solution)/shard_map/ppermute | solution.py:42
  74.9 0.1 collective-permute-start.12
  75.0 0.3 collective-permute-start.13
  75.4 0.8 collective-permute-done.12
  76.2 5.3 %collective-permute-done.13 = f32[8,256]{1,0:T(8,128)S(1)} collective-permute-done((f32[8,256]{1,0:T(8,128)S(1)}, f32[8,256]{1,0:T(8,128)S(1)}, u32[]{:S(2)}, u32[]{:S(2)}) %collective-permute-start.13) | collective-permute-done | bytes 8224 | tf_op jit(solution)/shard_map/ppermute | solution.py:32
  81.5 0.3 collective-permute-start.14
  81.9 6.1 %collective-permute-done.14.v0_ref = f32[8,256]{1,0:T(8,128)S(1)} collective-permute-done((f32[8,256]{1,0:T(8,128)S(1)}, f32[8,256]{1,0:T(8,128)S(1)}, u32[]{:S(2)}, u32[]{:S(2)}) %collective-permute-start.14) | collective-permute-done | bytes 8224 | tf_op jit(solution)/shard_map/ppermute | solution.py:32
  88.0 6.2 %shard_map.77 = (f32[24,256]{1,0:T(8,128)S(1)}, f32[512,128]{1,0:T(8,128)}, f32[2,256]{1,0:T(2,128)}) custom-call(s32[2]{0:T(128)S(1)} %copy-done.2, s32[2,16]{1,0:T(2,128)S(1)} %fusion.24.tab_ref, f32[8,256]{1,0:T(8,128)S(1)} %collective-permute-done.14.v0_ref, f32[8,256]{1,0:T(8,128)S(1)} %negate_add_fusion.2.v1_ref, ...), custom_call_target="tpu_custom_call" | custom-call | tf_op jit(solution)/shard_map/pallas_call | solution.py:249
  94.2 3.8 %collective-permute-done.16 = f32[24,256]{1,0:T(8,128)S(1)} collective-permute-done((f32[24,256]{1,0:T(8,128)S(1)}, f32[24,256]{1,0:T(8,128)S(1)}, u32[]{:S(2)}, u32[]{:S(2)}) %collective-permute-start.16) | collective-permute-done | bytes 24608 | tf_op jit(solution)/shard_map/ppermute | solution.py:42
  98.0 0.1 collective-permute-start.17
  98.2 5.0 %collective-permute-done.17 = f32[24,256]{1,0:T(8,128)S(1)} collective-permute-done((f32[24,256]{1,0:T(8,128)S(1)}, f32[24,256]{1,0:T(8,128)S(1)}, u32[]{:S(2)}, u32[]{:S(2)}) %collective-permute-start.17) | collective-permute-done | bytes 24608 | tf_op jit(solution)/shard_map/ppermute | solution.py:42
  103.2 0.1 collective-permute-start.18
  103.3 0.1 collective-permute-start.19
  103.4 1.1 collective-permute-done.18
  104.5 5.3 %collective-permute-done.19 = f32[8,256]{1,0:T(8,128)S(1)} collective-permute-done((f32[8,256]{1,0:T(8,128)S(1)}, f32[8,256]{1,0:T(8,128)S(1)}, u32[]{:S(2)}, u32[]{:S(2)}) %collective-permute-start.19) | collective-permute-done | bytes 8224 | tf_op jit(solution)/shard_map/ppermute | solution.py:32
  109.8 0.1 collective-permute-start.20
  109.9 0.1 collective-permute-start.21
  110.0 6.3 %collective-permute-done.20.v0_ref = f32[8,256]{1,0:T(8,128)S(1)} collective-permute-done((f32[8,256]{1,0:T(8,128)S(1)}, f32[8,256]{1,0:T(8,128)S(1)}, u32[]{:S(2)}, u32[]{:S(2)}) %collective-permute-start.20) | collective-permute-done | bytes 8224 | tf_op jit(solution)/shard_map/ppermute | solution.py:32
  116.3 5.4 %shard_map.78 = (f32[24,256]{1,0:T(8,128)S(1)}, f32[512,128]{1,0:T(8,128)S(1)}, f32[2,256]{1,0:T(2,128)S(1)}) custom-call(s32[2]{0:T(128)S(1)} %copy-done.2, s32[2,16]{1,0:T(2,128)S(1)} %fusion.24.tab_ref, f32[8,256]{1,0:T(8,128)S(1)} %collective-permute-done.20.v0_ref, f32[8,256]{1,0:T(8,128)S(1)} %negate_add_fusion.1.v1_ref, ...), custom_call_target="tpu_custom_call" | custom-call | tf_op jit(solution)/shard_map/pallas_call | solution.py:249
  121.8 0.1 collective-permute-start.22
  121.9 3.8 %collective-permute-done.22 = f32[24,256]{1,0:T(8,128)S(1)} collective-permute-done((f32[24,256]{1,0:T(8,128)S(1)}, f32[24,256]{1,0:T(8,128)S(1)}, u32[]{:S(2)}, u32[]{:S(2)}) %collective-permute-start.22) | collective-permute-done | bytes 24608 | tf_op jit(solution)/shard_map/ppermute | solution.py:42
  125.7 0.1 collective-permute-start.23
  125.8 5.0 %collective-permute-done.23 = f32[24,256]{1,0:T(8,128)S(1)} collective-permute-done((f32[24,256]{1,0:T(8,128)S(1)}, f32[24,256]{1,0:T(8,128)S(1)}, u32[]{:S(2)}, u32[]{:S(2)}) %collective-permute-start.23) | collective-permute-done | bytes 24608 | tf_op jit(solution)/shard_map/ppermute | solution.py:42
  130.9 0.1 collective-permute-start.24
  131.0 0.1 collective-permute-start.25
  131.1 0.2 multiply_reduce_fusion
  131.3 0.9 collective-permute-done.24
  132.2 5.3 %collective-permute-done.25 = f32[8,256]{1,0:T(8,128)S(1)} collective-permute-done((f32[8,256]{1,0:T(8,128)S(1)}, f32[8,256]{1,0:T(8,128)S(1)}, u32[]{:S(2)}, u32[]{:S(2)}) %collective-permute-start.25) | collective-permute-done | bytes 8224 | tf_op jit(solution)/shard_map/ppermute | solution.py:32
  137.5 0.1 collective-permute-start.26
  137.6 0.1 collective-permute-start.27
  137.7 0.6 add_multiply_fusion.3
  138.3 0.6 copy.9
  138.9 5.1 %collective-permute-done.26.v0_ref = f32[8,256]{1,0:T(8,128)S(1)} collective-permute-done((f32[8,256]{1,0:T(8,128)S(1)}, f32[8,256]{1,0:T(8,128)S(1)}, u32[]{:S(2)}, u32[]{:S(2)}) %collective-permute-start.26) | collective-permute-done | bytes 8224 | tf_op jit(solution)/shard_map/ppermute | solution.py:32
  144.0 7.0 %shard_map.79 = f32[512,512]{1,0:T(8,128)} custom-call(s32[2]{0:T(128)S(1)} %copy-done.2, s32[2,16]{1,0:T(2,128)S(1)} %fusion.24.tab_ref, f32[8,256]{1,0:T(8,128)S(1)} %collective-permute-done.26.v0_ref, f32[8,256]{1,0:T(8,128)S(1)} %get-tuple-element.22.v1_ref, f32[8,256]{1,0:T(8,128)S(1)} %collective-permute-done.27.v2_ref, ...), custom_call_target="tpu_custom_call" | custom-call | tf_op jit(solution)/shard_map/pallas_call | solution.py:268
  (44 shorter events, 0.5 us)
Async XLA Ops:
  0.6 51.8 %copy-start.1 = (bf16[2048,128]{1,0:T(8,128)(2,1)S(1)}, bf16[2048,128]{1,0:T(8,128)(2,1)}, u32[]{:S(2)}) copy-start(bf16[2048,128]{1,0:T(8,128)(2,1)} %refs_4_.1) | copy-start | bytes 1572868
  0.6 51.8 %copy-start = (bf16[512,512]{1,0:T(8,128)(2,1)S(1)}, bf16[512,512]{1,0:T(8,128)(2,1)}, u32[]{:S(2)}) copy-start(bf16[512,512]{1,0:T(8,128)(2,1)} %sim_ref.3) | copy-start | bytes 1572868
  0.7 51.8 %copy-start.2 = (s32[2]{0:T(128)S(1)}, s32[2]{0:T(128)}, u32[]{:S(2)}) copy-start(s32[2]{0:T(128)} %cnt_ref.7) | copy-start | bytes 28
  0.7 13.2 %collective-permute-start.1 = (bf16[2048,128]{1,0:T(8,128)(2,1)}, bf16[2048,128]{1,0:T(8,128)(2,1)S(1)}, u32[]{:S(2)}, u32[]{:S(2)}) collective-permute-start(bf16[2048,128]{1,0:T(8,128)(2,1)} %refs_4_.1), channel_id=1, source_target_pairs={{0,1},{1,2},{2,3},{3,0},{4,5},{5,6},{6,7},{7,4},{8,9},{9,10},{10,1... | collective-permute-start | bytes 1572872 | tf_op jit(solution)/shard_map/ppermute | solution.py:37
  0.8 13.7 %collective-permute-start.2 = (bf16[2048,128]{1,0:T(8,128)(2,1)}, bf16[2048,128]{1,0:T(8,128)(2,1)S(1)}, u32[]{:S(2)}, u32[]{:S(2)}) collective-permute-start(bf16[2048,128]{1,0:T(8,128)(2,1)} %refs_4_.1), channel_id=1, source_target_pairs={{0,3},{1,0},{2,1},{3,2},{4,7},{5,4},{6,5},{7,6},{8,11},{9,8},{10,9... | collective-permute-start | bytes 1572872 | tf_op jit(solution)/shard_map/ppermute | solution.py:37
  4.0 27.2 %collective-permute-start = (bf16[2048,128]{1,0:T(8,128)(2,1)}, bf16[2048,128]{1,0:T(8,128)(2,1)S(1)}, u32[]{:S(2)}, u32[]{:S(2)}) collective-permute-start(bf16[2048,128]{1,0:T(8,128)(2,1)} %refs_4_.1), channel_id=1, source_target_pairs={{0,252},{4,8},{8,4},{12,16},{16,12},{20,24},{24,20},{28,32},{32,28... | collective-permute-start | bytes 1572872 | tf_op jit(solution)/shard_map/ppermute | solution.py:32
  9.4 22.2 %collective-permute-start.7 = (bf16[2048,128]{1,0:T(8,128)(2,1)}, bf16[2048,128]{1,0:T(8,128)(2,1)}, u32[]{:S(2)}, u32[]{:S(2)}) collective-permute-start(bf16[2048,128]{1,0:T(8,128)(2,1)} %refs_4_.1), channel_id=1, source_target_pairs={{0,4},{4,0},{8,12},{12,8},{16,20},{20,16},{24,28},{28,24},{32,36},... | collective-permute-start | bytes 1572872 | tf_op jit(solution)/shard_map/ppermute | solution.py:27
  13.9 11.7 %collective-permute-start.4 = (bf16[1024,128]{1,0:T(8,128)(2,1)S(1)}, bf16[1024,128]{1,0:T(8,128)(2,1)S(1)}, u32[]{:S(2)}, u32[]{:S(2)}) collective-permute-start(bf16[1024,128]{1,0:T(8,128)(2,1)S(1)} %slice.62), channel_id=1, source_target_pairs={{0,1},{1,2},{2,3},{3,0},{4,5},{5,6},{6,7},{7,4},{8,9},{9,10},{10,1... | collective-permute-start | bytes 786440 | tf_op jit(solution)/shard_map/ppermute | solution.py:37
  14.5 11.2 %collective-permute-start.5 = (bf16[1024,128]{1,0:T(8,128)(2,1)S(1)}, bf16[1024,128]{1,0:T(8,128)(2,1)S(1)}, u32[]{:S(2)}, u32[]{:S(2)}) collective-permute-start(bf16[1024,128]{1,0:T(8,128)(2,1)S(1)} %slice.63), channel_id=1, source_target_pairs={{0,3},{1,0},{2,1},{3,2},{4,7},{5,4},{6,5},{7,6},{8,11},{9,8},{10,9... | collective-permute-start | bytes 786440 | tf_op jit(solution)/shard_map/ppermute | solution.py:37
  18.4 27.7 %collective-permute-start.3 = (bf16[2,2048,128]{2,1,0:T(8,128)(2,1)}, bf16[2,2048,128]{2,1,0:T(8,128)(2,1)}, u32[]{:S(2)}, u32[]{:S(2)}) collective-permute-start(bf16[2,2048,128]{2,1,0:T(8,128)(2,1)} %pad_maximum_fusion), channel_id=1, source_target_pairs={{0,252},{4,8},{8,4},{12,16},{16,12},{20,24},{24,20},{28,32},{32,28... | collective-permute-start | bytes 3145736 | tf_op jit(solution)/shard_map/ppermute | solution.py:32
  25.6 22.4 %collective-permute-start.8 = (bf16[2,2048,128]{2,1,0:T(8,128)(2,1)}, bf16[2,2048,128]{2,1,0:T(8,128)(2,1)}, u32[]{:S(2)}, u32[]{:S(2)}) collective-permute-start(bf16[2,2048,128]{2,1,0:T(8,128)(2,1)} %pad_maximum_fusion), channel_id=1, source_target_pairs={{0,4},{4,0},{8,12},{12,8},{16,20},{20,16},{24,28},{28,24},{32,36},... | collective-permute-start | bytes 3145736 | tf_op jit(solution)/shard_map/ppermute | solution.py:27
  25.8 17.5 %collective-permute-start.6 = (bf16[2048,128]{1,0:T(8,128)(2,1)S(1)}, bf16[2048,128]{1,0:T(8,128)(2,1)}, u32[]{:S(2)}, u32[]{:S(2)}) collective-permute-start(bf16[2048,128]{1,0:T(8,128)(2,1)S(1)} %constant_dynamic-update-slice_fusion.refs_7_), channel_id=1, source_target_pairs={{0,252},{4,8},{8,4},{12,16},{16,12},{20,24},{24,20},{28,32},{32,28... | collective-permute-start | bytes 1572872 | tf_op jit(solution)/shard_map/ppermute | solution.py:32
  31.5 13.2 %collective-permute-start.9 = (bf16[2048,128]{1,0:T(8,128)(2,1)S(1)}, bf16[2048,128]{1,0:T(8,128)(2,1)}, u32[]{:S(2)}, u32[]{:S(2)}) collective-permute-start(bf16[2048,128]{1,0:T(8,128)(2,1)S(1)} %constant_dynamic-update-slice_fusion.refs_7_), channel_id=1, source_target_pairs={{0,4},{4,0},{8,12},{12,8},{16,20},{20,16},{24,28},{28,24},{32,36},... | collective-permute-start | bytes 1572872 | tf_op jit(solution)/shard_map/ppermute | solution.py:27
  65.8 3.9 %collective-permute-start.10 = (f32[24,256]{1,0:T(8,128)S(1)}, f32[24,256]{1,0:T(8,128)S(1)}, u32[]{:S(2)}, u32[]{:S(2)}) collective-permute-start(f32[24,256]{1,0:T(8,128)S(1)} %get-tuple-element.10), channel_id=1, source_target_pairs={{0,1},{1,0},{2,3},{3,2},{4,5},{5,4},{6,7},{7,6},{8,9},{9,8},{10,11... | collective-permute-start | bytes 73736 | tf_op jit(solution)/shard_map/ppermute | solution.py:42
  69.8 5.1 %collective-permute-start.11 = (f32[24,256]{1,0:T(8,128)S(1)}, f32[24,256]{1,0:T(8,128)S(1)}, u32[]{:S(2)}, u32[]{:S(2)}) collective-permute-start(f32[24,256]{1,0:T(8,128)S(1)} %multiply_add_fusion.5), channel_id=1, source_target_pairs={{0,3},{1,2},{2,1},{3,0},{4,7},{5,6},{6,5},{7,4},{8,11},{9,10},{10,... | collective-permute-start | bytes 73736 | tf_op jit(solution)/shard_map/ppermute | solution.py:42
  74.9 1.3 collective-permute-start.12
  75.0 6.5 %collective-permute-start.13 = (f32[8,256]{1,0:T(8,128)S(1)}, f32[8,256]{1,0:T(8,128)S(1)}, u32[]{:S(2)}, u32[]{:S(2)}) collective-permute-start(f32[8,256]{1,0:T(8,128)S(1)} %get-tuple-element.32), channel_id=1, source_target_pairs={{0,252},{4,8},{8,4},{12,16},{16,12},{20,24},{24,20},{28,32},{32,28... | collective-permute-start | bytes 24584 | tf_op jit(solution)/shard_map/ppermute | solution.py:32
  81.5 6.5 %collective-permute-start.14 = (f32[8,256]{1,0:T(8,128)S(1)}, f32[8,256]{1,0:T(8,128)S(1)}, u32[]{:S(2)}, u32[]{:S(2)}) collective-permute-start(f32[8,256]{1,0:T(8,128)S(1)} %negate_add_fusion.2.v1_ref), channel_id=1, source_target_pairs={{0,252},{4,8},{8,4},{12,16},{16,12},{20,24},{24,20},{28,32},{32,28... | collective-permute-start | bytes 24584 | tf_op jit(solution)/shard_map/ppermute | solution.py:32
  81.9 6.1 %collective-permute-start.15 = (f32[8,256]{1,0:T(8,128)S(1)}, f32[8,256]{1,0:T(8,128)S(1)}, u32[]{:S(2)}, u32[]{:S(2)}) collective-permute-start(f32[8,256]{1,0:T(8,128)S(1)} %negate_add_fusion.2.v1_ref), channel_id=1, source_target_pairs={{0,4},{4,0},{8,12},{12,8},{16,20},{20,16},{24,28},{28,24},{32,36},... | collective-permute-start | bytes 24584 | tf_op jit(solution)/shard_map/ppermute | solution.py:27
  94.2 3.8 %collective-permute-start.16 = (f32[24,256]{1,0:T(8,128)S(1)}, f32[24,256]{1,0:T(8,128)S(1)}, u32[]{:S(2)}, u32[]{:S(2)}) collective-permute-start(f32[24,256]{1,0:T(8,128)S(1)} %get-tuple-element.12), channel_id=1, source_target_pairs={{0,1},{1,0},{2,3},{3,2},{4,5},{5,4},{6,7},{7,6},{8,9},{9,8},{10,11... | collective-permute-start | bytes 73736 | tf_op jit(solution)/shard_map/ppermute | solution.py:42
  98.0 5.1 %collective-permute-start.17 = (f32[24,256]{1,0:T(8,128)S(1)}, f32[24,256]{1,0:T(8,128)S(1)}, u32[]{:S(2)}, u32[]{:S(2)}) collective-permute-start(f32[24,256]{1,0:T(8,128)S(1)} %multiply_add_fusion.3), channel_id=1, source_target_pairs={{0,3},{1,2},{2,1},{3,0},{4,7},{5,6},{6,5},{7,4},{8,11},{9,10},{10,... | collective-permute-start | bytes 73736 | tf_op jit(solution)/shard_map/ppermute | solution.py:42
  103.2 1.3 collective-permute-start.18
  103.3 6.5 %collective-permute-start.19 = (f32[8,256]{1,0:T(8,128)S(1)}, f32[8,256]{1,0:T(8,128)S(1)}, u32[]{:S(2)}, u32[]{:S(2)}) collective-permute-start(f32[8,256]{1,0:T(8,128)S(1)} %get-tuple-element.30), channel_id=1, source_target_pairs={{0,252},{4,8},{8,4},{12,16},{16,12},{20,24},{24,20},{28,32},{32,28... | collective-permute-start | bytes 24584 | tf_op jit(solution)/shard_map/ppermute | solution.py:32
  109.8 6.5 %collective-permute-start.20 = (f32[8,256]{1,0:T(8,128)S(1)}, f32[8,256]{1,0:T(8,128)S(1)}, u32[]{:S(2)}, u32[]{:S(2)}) collective-permute-start(f32[8,256]{1,0:T(8,128)S(1)} %negate_add_fusion.1.v1_ref), channel_id=1, source_target_pairs={{0,252},{4,8},{8,4},{12,16},{16,12},{20,24},{24,20},{28,32},{32,28... | collective-permute-start | bytes 24584 | tf_op jit(solution)/shard_map/ppermute | solution.py:32
  109.9 6.4 %collective-permute-start.21 = (f32[8,256]{1,0:T(8,128)S(1)}, f32[8,256]{1,0:T(8,128)S(1)}, u32[]{:S(2)}, u32[]{:S(2)}) collective-permute-start(f32[8,256]{1,0:T(8,128)S(1)} %negate_add_fusion.1.v1_ref), channel_id=1, source_target_pairs={{0,4},{4,0},{8,12},{12,8},{16,20},{20,16},{24,28},{28,24},{32,36},... | collective-permute-start | bytes 24584 | tf_op jit(solution)/shard_map/ppermute | solution.py:27
  121.8 3.9 %collective-permute-start.22 = (f32[24,256]{1,0:T(8,128)S(1)}, f32[24,256]{1,0:T(8,128)S(1)}, u32[]{:S(2)}, u32[]{:S(2)}) collective-permute-start(f32[24,256]{1,0:T(8,128)S(1)} %get-tuple-element.13), channel_id=1, source_target_pairs={{0,1},{1,0},{2,3},{3,2},{4,5},{5,4},{6,7},{7,6},{8,9},{9,8},{10,11... | collective-permute-start | bytes 73736 | tf_op jit(solution)/shard_map/ppermute | solution.py:42
  125.7 5.1 %collective-permute-start.23 = (f32[24,256]{1,0:T(8,128)S(1)}, f32[24,256]{1,0:T(8,128)S(1)}, u32[]{:S(2)}, u32[]{:S(2)}) collective-permute-start(f32[24,256]{1,0:T(8,128)S(1)} %multiply_add_fusion.1), channel_id=1, source_target_pairs={{0,3},{1,2},{2,1},{3,0},{4,7},{5,6},{6,5},{7,4},{8,11},{9,10},{10,... | collective-permute-start | bytes 73736 | tf_op jit(solution)/shard_map/ppermute | solution.py:42
  130.9 1.3 collective-permute-start.24
  131.0 6.5 %collective-permute-start.25 = (f32[8,256]{1,0:T(8,128)S(1)}, f32[8,256]{1,0:T(8,128)S(1)}, u32[]{:S(2)}, u32[]{:S(2)}) collective-permute-start(f32[8,256]{1,0:T(8,128)S(1)} %get-tuple-element.28), channel_id=1, source_target_pairs={{0,252},{4,8},{8,4},{12,16},{16,12},{20,24},{24,20},{28,32},{32,28... | collective-permute-start | bytes 24584 | tf_op jit(solution)/shard_map/ppermute | solution.py:32
  137.5 6.5 %collective-permute-start.26 = (f32[8,256]{1,0:T(8,128)S(1)}, f32[8,256]{1,0:T(8,128)S(1)}, u32[]{:S(2)}, u32[]{:S(2)}) collective-permute-start(f32[8,256]{1,0:T(8,128)S(1)} %get-tuple-element.22.v1_ref), channel_id=1, source_target_pairs={{0,252},{4,8},{8,4},{12,16},{16,12},{20,24},{24,20},{28,32},{32,28... | collective-permute-start | bytes 24584 | tf_op jit(solution)/shard_map/ppermute | solution.py:32
  137.6 6.4 %collective-permute-start.27 = (f32[8,256]{1,0:T(8,128)S(1)}, f32[8,256]{1,0:T(8,128)S(1)}, u32[]{:S(2)}, u32[]{:S(2)}) collective-permute-start(f32[8,256]{1,0:T(8,128)S(1)} %get-tuple-element.22.v1_ref), channel_id=1, source_target_pairs={{0,4},{4,0},{8,12},{12,8},{16,20},{20,16},{24,28},{28,24},{32,36},... | collective-permute-start | bytes 24584 | tf_op jit(solution)/shard_map/ppermute | solution.py:27
